TPU v7x, 32 devices: a whole 2x2x4 slice. The times are simulated.
32 devices in a mesh: groups: 2 (over y), inst: 8 (over z, x), tensor: 2 (over core).
Axes of the slice: x: 2, y: 2, z: 4, core: 2. Of those that a mesh axis runs over, the one named last changes fastest.
Arguments:
- hidden: bfloat16 [2048, 2560], P(('groups', 'inst'), 'tensor'), parts along dimension 0, may hold values from -6 to 6
- value_weight: bfloat16 [2560, 512], P('tensor'), may hold values from -0.125 to 0.125
- adapter_down: bfloat16 [1024, 2560], P(('groups', 'inst', 'tensor')), parts along dimension 0, may hold values from -0.125 to 0.125
- adapter_up: bfloat16 [1024, 512], P(('groups', 'inst', 'tensor')), parts along dimension 0, may hold values from -0.75 to 0.75
- block_adapter: int32 [16], P('groups'), parts along dimension 0, may hold values from 0 to 7
- queries: bfloat16 [2048, 4096], P(('groups', 'inst'), 'tensor'), parts along dimension 0, may hold values from -65 to 65
- new_keys: bfloat16 [2048, 512], P(('groups', 'inst'), 'tensor'), parts along dimension 0, may hold values from -5 to 5
- kv_pool: bfloat16 [3072, 16, 1024], P(('groups', 'inst'), None, 'tensor'), parts along dimension 0, may hold values from -6 to 6
- page_request: int32 [3072], P(('groups', 'inst')), parts along dimension 0, may hold values from -1 to 7
- page_pos: int32 [3072], P(('groups', 'inst')), parts along dimension 0, may hold values from 0 to 255
- token_request: int32 [2048], P(('groups', 'inst')), parts along dimension 0, may hold values from 0 to 7
- token_pos: int32 [2048], P(('groups', 'inst')), parts along dimension 0, may hold values from 0 to 4095
- send_page: int32 [96], P(('groups', 'inst')), parts along dimension 0, may hold values from 0 to 191, as said below
- send_dest: int32 [96], P(('groups', 'inst')), parts along dimension 0, may hold values from 0 to 7, as said below
- dest_slot: int32 [96], P(('groups', 'inst')), parts along dimension 0, may hold values from 0 to 191, as said below
- send_count: int32 [16], P(('groups', 'inst')), parts along dimension 0, may hold values from 3 to 6, as said below
Outputs:
- attended: bfloat16 [2048, 4096], P(('groups', 'inst'), 'tensor'), parts along dimension 0
- new_values: bfloat16 [2048, 512], P(('groups', 'inst'), 'tensor'), parts along dimension 0
There are 2 independent parts, one for each index of `groups`. A program takes and returns all parts, laid end to end along the dimension named above; an argument that names none is the same for every part. Nothing has to cross between parts.
Inputs may be any that keep to these rules, and one draw needn't show every extreme that they name: Page slots of one instance in send_page are distinct, and differ from all slots named for that instance in dest_slot. `send_dest`: the entries of one instance name 6 different instances other than itself, and every instance is named by exactly one entry of each position k of the lists. `dest_slot`: no receiver slot is named twice. `send_count`: some instance has 6 live entries.
All inputs are finite; a program needn't handle non-finite values.
Results may differ from a plain program's by a relative error of at most 0.0043.
Values may be sent and summed in bfloat16 or wider, within the bound.
A program may use at most 128 MiB of HBM per device.

v0:
```python
import functools
import math

import jax
import jax.numpy as jnp
from jax import lax
from jax.experimental import pallas as pl
from jax.experimental.pallas import tpu as pltpu
from jax.sharding import PartitionSpec as P

HD = 128
FAR = -1e30
F32 = jnp.float32
BF16 = jnp.bfloat16
MESH = pl.DeviceIdType.MESH


def dot(a, b):
    return jnp.dot(a, b, preferred_element_type=F32)


def dot_t(a, b):
    return lax.dot_general(a, b, (((1,), (1,)), ((), ())), preferred_element_type=F32)


def kernel(
    inst,
    block_adapter,
    send_page,
    send_dest,
    dest_slot,
    send_count,
    page_info,
    token_info,
    hidden,
    weight,
    down,
    up,
    queries,
    new_keys,
    pool,
    attended,
    new_values,
    stage1,
    recv1,
    stage2,
    recv2,
    out_pages,
    in_pages,
    out_slots,
    in_slots,
    hid_other,
    down_f,
    up_f,
    combined,
    recvc,
    q3,
    vaug,
    bias,
    bias2,
    k2,
    v2,
    acc,
    top,
    one_send,
    one_recv,
    two_send,
    two_recv,
    page_send,
    page_recv,
    slot_send,
    slot_recv,
    pair_send,
    pair_recv,
):
    me = lax.axis_index("inst")
    t = lax.axis_index("tensor")
    other = 1 - t
    tokens = hidden.shape[0]
    feats = hidden.shape[1]
    rank = down.shape[0]
    pages, page_tokens, _ = pool.shape
    keys = pages * page_tokens
    heads = q3.shape[0]
    groups = new_keys.shape[1] // HD
    per = heads // groups
    vals = groups * HD
    mig = send_page.shape[0]
    slots = stage1.shape[1] // 16
    c = math.log2(math.e) / math.sqrt(HD)

    def peer(o):
        return lax.rem(me + o, inst)

    def source(o):
        return lax.rem(me - o + inst, inst)

    def each(body):
        lax.fori_loop(1, inst, lambda o, _: (body(o), 0)[1], 0)

    barrier = pltpu.get_barrier_semaphore()
    each(
        lambda o: pl.semaphore_signal(
            barrier, inc=1, device_id={"inst": peer(o)}, device_id_type=MESH
        )
    )
    pl.semaphore_signal(barrier, inc=1, device_id={"tensor": other}, device_id_type=MESH)

    def remote(src, dst, send, recv, o):
        return pltpu.make_async_remote_copy(
            src_ref=src,
            dst_ref=dst,
            send_sem=send.at[o],
            recv_sem=recv.at[o],
            device_id={"inst": peer(o)},
            device_id_type=MESH,
        )

    def paired(src, dst, k):
        return pltpu.make_async_remote_copy(
            src_ref=src,
            dst_ref=dst,
            send_sem=pair_send.at[k],
            recv_sem=pair_recv.at[k],
            device_id={"tensor": other},
            device_id_type=MESH,
        )

    slot_copy = lambda o: remote(out_slots.at[peer(o)], in_slots.at[me], slot_send, slot_recv, o)
    slot_in = lambda o: remote(
        out_slots.at[peer(o)], in_slots.at[source(o)], slot_send, slot_recv, o
    )
    page_copy = lambda o: remote(out_pages.at[peer(o)], in_pages.at[me], page_send, page_recv, o)
    page_in = lambda o: remote(
        out_pages.at[peer(o)], in_pages.at[source(o)], page_send, page_recv, o
    )
    one_copy = lambda o: remote(stage1.at[peer(o)], recv1.at[me], one_send, one_recv, o)
    one_in = lambda o: remote(stage1.at[peer(o)], recv1.at[source(o)], one_send, one_recv, o)
    two_copy = lambda o: remote(stage2.at[peer(o)], recv2.at[me], two_send, two_recv, o)
    two_in = lambda o: remote(stage2.at[peer(o)], recv2.at[source(o)], two_send, two_recv, o)

    cols = down.shape[1] // HD
    tiles = []
    for h in range(rank // 16):
        for k in range(cols):
            tiles.append((down, h, k))
    for h in range(rank // 16):
        for k in range(up.shape[1] // HD):
            tiles.append((up, h, k))
    for q, (ref, h, k) in enumerate(tiles):
        at = (q % slots) * 16
        stage1[q // slots, at : at + 16, :] = ref[h * 16 : h * 16 + 16, k * HD : (k + 1) * HD]
    for q in range(len(tiles), inst * slots):
        at = (q % slots) * 16
        stage1[q // slots, at : at + 16, :] = jnp.zeros((16, HD), BF16)

    count = send_count[0]

    def choose(j, _):
        def look(k, found):
            page, slot = found
            hit = (send_dest[k] == j) & (k < count)
            return jnp.where(hit, send_page[k], page), jnp.where(hit, dest_slot[k], slot)

        page, slot = lax.fori_loop(
            0, mig, look, (jnp.int32(0), jnp.int32(-1)), unroll=mig <= 8
        )
        out_slots[j] = jnp.full(out_slots.shape[1:], slot, jnp.int32)
        out_pages[j] = pool[page]
        return 0

    lax.fori_loop(0, inst, choose, 0)

    pl.semaphore_wait(barrier, inst)
    each(lambda o: slot_copy(o).start())
    each(lambda o: one_copy(o).start())
    paired(hidden, hid_other, 0).start()
    each(lambda o: page_copy(o).start())
    recv1[me] = stage1[me]
    in_slots[me] = jnp.full(in_slots.shape[1:], -1, jnp.int32)
    in_pages[me] = jnp.zeros(in_pages.shape[1:], BF16)

    base = dot(hidden[...], weight[...])
    for h in range(2):
        combined[h] = base[:, h * vals : (h + 1) * vals]
    for h in range(heads):
        q3[h] = queries[:, h * HD : (h + 1) * HD]
    for g in range(groups):
        vaug[g, :, :HD] = pool[:, :, (2 * g + 1) * HD : (2 * g + 2) * HD].reshape(keys, HD)
        vaug[g, :, HD:] = jnp.ones((keys, HD), BF16)
        v2[g, :, HD:] = jnp.ones((v2.shape[1], HD), BF16)

    t_row = token_info[...].astype(F32)
    t_req = jnp.broadcast_to(t_row[0:1], (tokens, tokens)).T[:, 0:1]
    t_pos = jnp.broadcast_to(t_row[1:2], (tokens, tokens)).T[:, 0:1]

    each(lambda o: slot_in(o).wait_recv())
    lane = lax.broadcasted_iota(jnp.int32, (1, HD), 1)
    info = page_info[...].astype(F32)
    page_col = lax.broadcasted_iota(jnp.int32, (pages, HD), 0)
    gone = jnp.zeros((8, pages), F32)
    per_row = HD // page_tokens
    for b in range(inst // per_row):
        row = jnp.full((1, HD), -1, jnp.int32)
        for j in range(per_row):
            row = jnp.where(lane // page_tokens == j, in_slots[b * per_row + j][0:1], row)
        match = (page_col == row).astype(F32).astype(BF16)
        gone = gone + dot_t(jnp.ones((8, HD), BF16), match)
        found = dot(info.astype(BF16), match)
        req = jnp.where(row >= 0, found[0:1], -2.0)
        at = found[1:2] * page_tokens + (lane % page_tokens).astype(F32)
        ok = (req == t_req) & (at <= t_pos)
        bias2[:, b * HD : (b + 1) * HD] = jnp.where(ok, 0.0, FAR)
    ok = (t_row[0:1] == t_req) & (t_row[1:2] <= t_pos)
    bias2[:, inst * page_tokens :] = jnp.where(ok, 0.0, FAR)
    first = lax.broadcasted_iota(jnp.int32, (8, pages), 0) == 0
    info = jnp.where(first & (gone > 0.5), -1.0, info).astype(BF16)
    spread_page = lax.broadcasted_iota(jnp.int32, (pages, keys), 0)
    spread_key = lax.broadcasted_iota(jnp.int32, (pages, keys), 1) // page_tokens
    spread = (spread_page == spread_key).astype(F32).astype(BF16)
    key_info = dot(info, spread)
    entry = lax.broadcasted_iota(jnp.int32, (1, keys), 1) % page_tokens
    key_at = key_info[1:2] * page_tokens + entry.astype(F32)
    ok = (key_info[0:1] == t_req) & (key_at <= t_pos)
    bias[...] = jnp.where(ok, 0.0, FAR)

    each(lambda o: one_in(o).wait_recv())

    def pick(j, _):
        stage2[j] = recv1[block_adapter[j]]
        return 0

    lax.fori_loop(0, inst, pick, 0)
    each(lambda o: two_copy(o).start())
    recv2[me] = stage2[me]

    both = 2

    def pool_part(g):
        def step(i, _):
            h = g * per + i * both
            q = q3[pl.ds(h, both)].reshape(both * tokens, HD)
            k = pool[:, :, 2 * g * HD : (2 * g + 1) * HD].reshape(keys, HD)
            s = dot_t(q, k).reshape(both, tokens, keys) + bias[...][None]
            m = jnp.max(s, axis=-1, keepdims=True)
            p = jnp.exp2((s - m) * c).astype(BF16).reshape(both * tokens, keys)
            acc[pl.ds(h, both)] = dot(p, vaug[g]).reshape(both, tokens, 2 * HD)
            top[pl.ds(h, both)] = jnp.broadcast_to(m, (both, tokens, HD))
            return 0

        lax.fori_loop(0, per // both, step, 0)

    half = groups // 2
    for g in range(half):
        pool_part(g)

    each(lambda o: two_in(o).wait_recv())
    paired(hidden, hid_other, 0).wait_recv()
    for q, (ref, h, k) in enumerate(tiles):
        at = (q % slots) * 16
        tile = recv2[q // slots, at : at + 16, :]
        if ref is down:
            side, col = divmod(k * HD, feats)
            down_f[side, h * 16 : h * 16 + 16, col : col + HD] = tile
        else:
            up_f[h * 16 : h * 16 + 16, k * HD : (k + 1) * HD] = tile
    low = dot_t(hidden[...], down_f[t]) + dot_t(hid_other[...], down_f[other])
    delta = jnp.zeros((tokens, up.shape[1]), F32)
    for _ in range(3):
        part = low.astype(BF16)
        low = low - part.astype(F32)
        delta = delta + dot(part, up_f[...])
    for h in range(2):
        combined[h] = combined[h] + delta[:, h * vals : (h + 1) * vals]
    paired(combined.at[other], recvc, 1).start()

    for g in range(half, groups):
        pool_part(g)

    paired(combined.at[other], recvc, 1).wait_recv()
    each(lambda o: page_in(o).wait_recv())
    values = (combined[t] + recvc[...]).astype(BF16)
    new_values[...] = values
    arrived = inst * page_tokens
    for g in range(groups):
        k2[g, :arrived, :] = in_pages[:, :, 2 * g * HD : (2 * g + 1) * HD].reshape(arrived, HD)
        k2[g, arrived:, :] = new_keys[:, g * HD : (g + 1) * HD]
        v2[g, :arrived, :HD] = in_pages[:, :, (2 * g + 1) * HD : (2 * g + 2) * HD].reshape(
            arrived, HD
        )
        v2[g, arrived:, :HD] = values[:, g * HD : (g + 1) * HD]
    for h in range(0, heads, both):
        g = h // per
        q = q3[h : h + both].reshape(both * tokens, HD)
        s = dot_t(q, k2[g]).reshape(both, tokens, k2.shape[1]) + bias2[...][None]
        m_old = top[h : h + both][:, :, 0:1]
        m = jnp.maximum(jnp.max(s, axis=-1, keepdims=True), m_old)
        p = jnp.exp2((s - m) * c).astype(BF16).reshape(both * tokens, k2.shape[1])
        keep = jnp.exp2((m_old - m) * c)
        whole = acc[h : h + both] * keep + dot(p, v2[g]).reshape(both, tokens, 2 * HD)
        done = (whole[:, :, :HD] / whole[:, :, HD:]).astype(BF16)
        for k in range(both):
            attended[:, (h + k) * HD : (h + k + 1) * HD] = done[k]

    each(lambda o: slot_copy(o).wait_send())
    each(lambda o: one_copy(o).wait_send())
    each(lambda o: two_copy(o).wait_send())
    each(lambda o: page_copy(o).wait_send())
    paired(hidden, hid_other, 0).wait_send()
    paired(combined.at[other], recvc, 1).wait_send()


def shards(
    hidden,
    value_weight,
    adapter_down,
    adapter_up,
    block_adapter,
    queries,
    new_keys,
    kv_pool,
    page_request,
    page_pos,
    token_request,
    token_pos,
    send_page,
    send_dest,
    dest_slot,
    send_count,
):
    inst = lax.axis_size("inst")
    tokens, feats = hidden.shape
    rank, wide = adapter_down.shape
    kv_cols = value_weight.shape[1]
    vals = new_keys.shape[1]
    groups = vals // HD
    heads = queries.shape[1] // HD
    pages, page_tokens, page_cols = kv_pool.shape
    keys = pages * page_tokens
    tiles = (rank // 16) * (wide + kv_cols) // HD
    slots = -(-tiles // inst)
    last = inst * page_tokens + tokens
    zero_p = jnp.zeros((6, pages), jnp.int32)
    page_info = jnp.concatenate([page_request[None], page_pos[None], zero_p], axis=0)
    zero_t = jnp.zeros((6, tokens), jnp.int32)
    token_info = jnp.concatenate([token_request[None], token_pos[None], zero_t], axis=0)
    smem = pl.BlockSpec(memory_space=pltpu.SMEM)
    vmem = pl.BlockSpec(memory_space=pltpu.VMEM)
    share = (inst, slots * 16, HD)
    out = pl.pallas_call(
        functools.partial(kernel, inst),
        out_shape=(
            jax.ShapeDtypeStruct((tokens, heads * HD), BF16),
            jax.ShapeDtypeStruct((tokens, vals), BF16),
        ),
        in_specs=[smem] * 5 + [vmem] * 9,
        out_specs=(vmem, vmem),
        scratch_shapes=[
            pltpu.VMEM(share, BF16),
            pltpu.VMEM(share, BF16),
            pltpu.VMEM(share, BF16),
            pltpu.VMEM(share, BF16),
            pltpu.VMEM((inst, page_tokens, page_cols), BF16),
            pltpu.VMEM((inst, page_tokens, page_cols), BF16),
            pltpu.VMEM((inst, 8, HD), jnp.int32),
            pltpu.VMEM((inst, 8, HD), jnp.int32),
            pltpu.VMEM((tokens, feats), BF16),
            pltpu.VMEM((2, rank, feats), BF16),
            pltpu.VMEM((rank, kv_cols), BF16),
            pltpu.VMEM((2, tokens, vals), F32),
            pltpu.VMEM((tokens, vals), F32),
            pltpu.VMEM((heads, tokens, HD), BF16),
            pltpu.VMEM((groups, keys, 2 * HD), BF16),
            pltpu.VMEM((tokens, keys), F32),
            pltpu.VMEM((tokens, last), F32),
            pltpu.VMEM((groups, last, HD), BF16),
            pltpu.VMEM((groups, last, 2 * HD), BF16),
            pltpu.VMEM((heads, tokens, 2 * HD), F32),
            pltpu.VMEM((heads, tokens, HD), F32),
        ]
        + [pltpu.SemaphoreType.DMA((inst,))] * 8
        + [pltpu.SemaphoreType.DMA((2,))] * 2,
        compiler_params=pltpu.CompilerParams(
            collective_id=0, has_side_effects=True, vmem_limit_bytes=56 * 1024 * 1024
        ),
        name="serve",
    )(
        block_adapter,
        send_page,
        send_dest,
        dest_slot,
        send_count,
        page_info,
        token_info,
        hidden,
        value_weight,
        adapter_down,
        adapter_up,
        queries,
        new_keys,
        kv_pool,
    )
    return out


def solution(mesh):
    placed = (
        P(("groups", "inst"), "tensor"),
        P("tensor", None),
        P(("groups", "inst", "tensor"), None),
        P(("groups", "inst", "tensor"), None),
        P("groups"),
        P(("groups", "inst"), "tensor"),
        P(("groups", "inst"), "tensor"),
        P(("groups", "inst"), None, "tensor"),
        P(("groups", "inst")),
        P(("groups", "inst")),
        P(("groups", "inst")),
        P(("groups", "inst")),
        P(("groups", "inst")),
        P(("groups", "inst")),
        P(("groups", "inst")),
        P(("groups", "inst")),
    )
    return jax.shard_map(
        shards,
        mesh=mesh,
        in_specs=placed,
        out_specs=(P(("groups", "inst"), "tensor"), P(("groups", "inst"), "tensor")),
        check_vma=False,
    )
```

profile of v0, /device:TPU:15, one launch (start us, length us, event | category | flops | bytes accessed | tf_op | source)
XLA Modules:
  0.0 43.1 jit_solution(14495944750434326822)
XLA Ops:
  1.3 0.1 pad.5.clone
  1.4 1.3 %add_add_fusion.1.token_info = s32[8,128]{1,0:T(8,128)} fusion(s32[1,128]{1,0:T(1,128)} %bitcast.6, s32[1,128]{1,0:T(1,128)} %bitcast.7, s32[8]{0:T(128)S(1)} %pad.5.clone), kind=kLoop, calls=%fused_computation.1 | loop fusion | flops 2048 | bytes 5152 | tf_op jit(solution)/shard_map/concatenate | solution.py:346
  2.7 1.4 %add_add_fusion.page_info = s32[8,192]{1,0:T(8,128)} fusion(s32[1,192]{1,0:T(1,128)} %bitcast.4, s32[1,192]{1,0:T(1,128)} %bitcast.5, s32[8]{0:T(128)S(1)} %pad.5.clone), kind=kLoop, calls=%fused_computation | loop fusion | flops 3072 | bytes 7712 | tf_op jit(solution)/shard_map/concatenate | solution.py:344
  4.1 35.7 %serve.1 = (bf16[128,2048]{1,0:T(8,128)(2,1)}, bf16[128,256]{1,0:T(8,128)(2,1)}) custom-call(s32[8]{0:T(128)} %block_adapter.1, s32[6]{0:T(128)} %send_page.1, s32[6]{0:T(128)} %send_dest.1, s32[6]{0:T(128)} %dest_slot.1, s32[1]{0:T(128)S(6)} %copy.20.send_count, s32[8,192]{1,0:T(8,128)} %add_add_fusion.page_info, s32[8,128]{1,0:T(8,128)} %add_add_fusion.1.token_info, ...), custom_call_target="tpu_custom_call" | custom-call | tf_op jit(solution)/shard_map/serve/pallas_call | solution.py:350
  39.7 1.9 %copy.21 = bf16[128,2048]{1,0:T(8,128)(2,1)} copy(bf16[128,2048]{1,0:T(8,128)(2,1)} %get-tuple-element.4) | data formatting | bytes 1048576
  41.6 1.5 %copy.22 = bf16[128,256]{1,0:T(8,128)(2,1)} copy(bf16[128,256]{1,0:T(8,128)(2,1)} %get-tuple-element.5) | data formatting | bytes 131072
  (1 shorter events, 0.0 us)
where the time goes:
time: 43.4 us; the launch traced here: 43.1 us
  Pallas kernels  35.7 us (82%)
  local copies, waits for them, and re-layouts  3.43 us (8%)
  other arithmetic  2.7 us (6%)
  between operations  1.29 us (3%)
    pallas_call x1, Pallas kernels, shards(): pl.pallas_call(functools.partial(kernel, inst), out_shape=(jax.ShapeDtype...  35.7 us
    unnamed x2, local copies, waits for them, and re-layouts  3.35 us
    concatenate x1, other arithmetic, shards(): jnp.concatenate([page_request[None], page_pos[None], zero_p], axis=0)  1.36 us
    concatenate x1, other arithmetic, shards(): jnp.concatenate([token_request[None], token_pos[None], zero_t], axis=0)  1.33 us

commit v1 on v0

--- a/solution.py
+++ b/solution.py
@@ -10,6 +10,8 @@
 
 HD = 128
 FAR = -1e30
+FIRST = 3
+SECOND = 6
 F32 = jnp.float32
 BF16 = jnp.bfloat16
 MESH = pl.DeviceIdType.MESH
@@ -25,22 +27,35 @@
 
 def kernel(
     inst,
+    *refs,
+):
+    sources, refs = refs[:16], refs[16:]
+    attended, new_values, refs = refs[0], refs[1], refs[2:]
+    places, refs = refs[:16], refs[16:]
+    run(inst, sources, attended, new_values, *places, *refs)
+
+
+def run(
+    inst,
+    sources,
+    attended,
+    new_values,
+    hidden,
+    weight,
+    down,
+    up,
     block_adapter,
+    queries,
+    new_keys,
+    pool,
+    page_request,
+    page_pos,
+    token_request,
+    token_pos,
     send_page,
     send_dest,
     dest_slot,
     send_count,
-    page_info,
-    token_info,
-    hidden,
-    weight,
-    down,
-    up,
-    queries,
-    new_keys,
-    pool,
-    attended,
-    new_values,
     stage1,
     recv1,
     stage2,
@@ -58,6 +73,7 @@
     vaug,
     bias,
     bias2,
+    spread,
     k2,
     v2,
     acc,
@@ -72,6 +88,7 @@
     slot_recv,
     pair_send,
     pair_recv,
+    local_sem,
 ):
     me = lax.axis_index("inst")
     t = lax.axis_index("tensor")
@@ -106,6 +123,29 @@
     )
     pl.semaphore_signal(barrier, inc=1, device_id={"tensor": other}, device_id_type=MESH)
 
+    order = [12, 13, 14, 15, 8, 9, 10, 11, 4, 2, 3, 7, 0, 1, 5, 6]
+    mine = (
+        hidden,
+        weight,
+        down,
+        up,
+        block_adapter,
+        queries,
+        new_keys,
+        pool,
+        page_request,
+        page_pos,
+        token_request,
+        token_pos,
+        send_page,
+        send_dest,
+        dest_slot,
+        send_count,
+    )
+    loads = [pltpu.make_async_copy(a, b, local_sem.at[k]) for k, (a, b) in enumerate(zip(sources, mine))]
+    for k in order:
+        loads[k].start()
+
     def remote(src, dst, send, recv, o):
         return pltpu.make_async_remote_copy(
             src_ref=src,
@@ -139,6 +179,8 @@
     two_copy = lambda o: remote(stage2.at[peer(o)], recv2.at[me], two_send, two_recv, o)
     two_in = lambda o: remote(stage2.at[peer(o)], recv2.at[source(o)], two_send, two_recv, o)
 
+    loads[2].wait()
+    loads[3].wait()
     cols = down.shape[1] // HD
     tiles = []
     for h in range(rank // 16):
@@ -154,6 +196,8 @@
         at = (q % slots) * 16
         stage1[q // slots, at : at + 16, :] = jnp.zeros((16, HD), BF16)
 
+    for k in (12, 13, 14, 15, 7):
+        loads[k].wait()
     count = send_count[0]
 
     def choose(j, _):
@@ -171,32 +215,50 @@
 
     lax.fori_loop(0, inst, choose, 0)
 
+    recv1[me] = stage1[me]
+    in_slots[me] = jnp.full(in_slots.shape[1:], -1, jnp.int32)
+    in_pages[me] = jnp.zeros(in_pages.shape[1:], BF16)
+    for k in (8, 9, 10, 11, 4, 0):
+        loads[k].wait()
+
+    t_reqs = token_request[...].astype(F32).reshape(1, tokens)
+    t_poss = token_pos[...].astype(F32).reshape(1, tokens)
+    t_req = jnp.broadcast_to(t_reqs, (tokens, tokens)).T[:, 0:1]
+    t_pos = jnp.broadcast_to(t_poss, (tokens, tokens)).T[:, 0:1]
+    ok = (t_reqs == t_req) & (t_poss <= t_pos)
+    bias2[:, inst * page_tokens :] = jnp.where(ok, 0.0, FAR)
+    owners = jnp.broadcast_to(page_request[...].astype(F32).reshape(1, pages), (8, pages))
+    indices = jnp.broadcast_to(page_pos[...].astype(F32).reshape(1, pages), (8, pages))
+    owners = owners.astype(BF16)
+    indices = indices.astype(BF16)
+    spread_page = lax.broadcasted_iota(jnp.int32, (pages, keys), 0)
+    spread_key = lax.broadcasted_iota(jnp.int32, (pages, keys), 1) // page_tokens
+    spread[...] = (spread_page == spread_key).astype(F32).astype(BF16)
+    entry = lax.broadcasted_iota(jnp.int32, (1, keys), 1) % page_tokens
+    key_at = dot(indices, spread[...])[0:1] * page_tokens + entry.astype(F32)
+    ok = (dot(owners, spread[...])[0:1] == t_req) & (key_at <= t_pos)
+    bias[...] = jnp.where(ok, 0.0, FAR)
+
     pl.semaphore_wait(barrier, inst)
     each(lambda o: slot_copy(o).start())
     each(lambda o: one_copy(o).start())
     paired(hidden, hid_other, 0).start()
-    each(lambda o: page_copy(o).start())
-    recv1[me] = stage1[me]
-    in_slots[me] = jnp.full(in_slots.shape[1:], -1, jnp.int32)
-    in_pages[me] = jnp.zeros(in_pages.shape[1:], BF16)
-
-    base = dot(hidden[...], weight[...])
-    for h in range(2):
-        combined[h] = base[:, h * vals : (h + 1) * vals]
+
+    for k in (1, 5, 6):
+        loads[k].wait()
     for h in range(heads):
         q3[h] = queries[:, h * HD : (h + 1) * HD]
     for g in range(groups):
         vaug[g, :, :HD] = pool[:, :, (2 * g + 1) * HD : (2 * g + 2) * HD].reshape(keys, HD)
         vaug[g, :, HD:] = jnp.ones((keys, HD), BF16)
         v2[g, :, HD:] = jnp.ones((v2.shape[1], HD), BF16)
-
-    t_row = token_info[...].astype(F32)
-    t_req = jnp.broadcast_to(t_row[0:1], (tokens, tokens)).T[:, 0:1]
-    t_pos = jnp.broadcast_to(t_row[1:2], (tokens, tokens)).T[:, 0:1]
+        k2[g, inst * page_tokens :, :] = new_keys[:, g * HD : (g + 1) * HD]
+    base = dot(hidden[...], weight[...])
+    for h in range(2):
+        combined[h] = base[:, h * vals : (h + 1) * vals]
 
     each(lambda o: slot_in(o).wait_recv())
     lane = lax.broadcasted_iota(jnp.int32, (1, HD), 1)
-    info = page_info[...].astype(F32)
     page_col = lax.broadcasted_iota(jnp.int32, (pages, HD), 0)
     gone = jnp.zeros((8, pages), F32)
     per_row = HD // page_tokens
@@ -206,24 +268,45 @@
             row = jnp.where(lane // page_tokens == j, in_slots[b * per_row + j][0:1], row)
         match = (page_col == row).astype(F32).astype(BF16)
         gone = gone + dot_t(jnp.ones((8, HD), BF16), match)
-        found = dot(info.astype(BF16), match)
-        req = jnp.where(row >= 0, found[0:1], -2.0)
-        at = found[1:2] * page_tokens + (lane % page_tokens).astype(F32)
+        req = jnp.where(row >= 0, dot(owners, match)[0:1], -2.0)
+        at = dot(indices, match)[0:1] * page_tokens + (lane % page_tokens).astype(F32)
         ok = (req == t_req) & (at <= t_pos)
         bias2[:, b * HD : (b + 1) * HD] = jnp.where(ok, 0.0, FAR)
-    ok = (t_row[0:1] == t_req) & (t_row[1:2] <= t_pos)
-    bias2[:, inst * page_tokens :] = jnp.where(ok, 0.0, FAR)
-    first = lax.broadcasted_iota(jnp.int32, (8, pages), 0) == 0
-    info = jnp.where(first & (gone > 0.5), -1.0, info).astype(BF16)
-    spread_page = lax.broadcasted_iota(jnp.int32, (pages, keys), 0)
-    spread_key = lax.broadcasted_iota(jnp.int32, (pages, keys), 1) // page_tokens
-    spread = (spread_page == spread_key).astype(F32).astype(BF16)
-    key_info = dot(info, spread)
-    entry = lax.broadcasted_iota(jnp.int32, (1, keys), 1) % page_tokens
-    key_at = key_info[1:2] * page_tokens + entry.astype(F32)
-    ok = (key_info[0:1] == t_req) & (key_at <= t_pos)
-    bias[...] = jnp.where(ok, 0.0, FAR)
-
+    gone = (gone > 0.5).astype(F32).astype(BF16)
+    lost = dot(gone, spread[...])[0:1] > 0.5
+    bias[...] = jnp.where(lost, FAR, bias[...])
+
+    both = 2
+
+    def pool_part(lo, hi):
+        def step(i, _):
+            h = i * both
+            g = h // per
+            q = q3[pl.ds(h, both)].reshape(both * tokens, HD)
+            lanes = pl.ds(pl.multiple_of(g * (2 * HD), 2 * HD), HD)
+            n = keys // 512
+            scored = []
+            m = None
+            for j in range(n):
+                k = pool[j * 512 // page_tokens : (j + 1) * 512 // page_tokens, :, lanes]
+                s = dot_t(q, k.reshape(512, HD)).reshape(both, tokens, 512)
+                s = s + bias[:, j * 512 : (j + 1) * 512][None]
+                part = jnp.max(s, axis=-1, keepdims=True)
+                m = part if m is None else jnp.maximum(m, part)
+                scored.append(s)
+            total = None
+            for j in range(n):
+                p = jnp.exp2((scored[j] - m) * c).astype(BF16).reshape(both * tokens, 512)
+                part = dot(p, vaug[g, j * 512 : (j + 1) * 512])
+                total = part if total is None else total + part
+            acc[pl.ds(h, both)] = total.reshape(both, tokens, 2 * HD)
+            top[pl.ds(h, both)] = jnp.broadcast_to(m, (both, tokens, HD))
+            return 0
+
+        lax.fori_loop(lo, hi, step, 0)
+
+    steps = heads // both
+    pool_part(0, FIRST)
     each(lambda o: one_in(o).wait_recv())
 
     def pick(j, _):
@@ -232,27 +315,9 @@
 
     lax.fori_loop(0, inst, pick, 0)
     each(lambda o: two_copy(o).start())
+    each(lambda o: page_copy(o).start())
     recv2[me] = stage2[me]
-
-    both = 2
-
-    def pool_part(g):
-        def step(i, _):
-            h = g * per + i * both
-            q = q3[pl.ds(h, both)].reshape(both * tokens, HD)
-            k = pool[:, :, 2 * g * HD : (2 * g + 1) * HD].reshape(keys, HD)
-            s = dot_t(q, k).reshape(both, tokens, keys) + bias[...][None]
-            m = jnp.max(s, axis=-1, keepdims=True)
-            p = jnp.exp2((s - m) * c).astype(BF16).reshape(both * tokens, keys)
-            acc[pl.ds(h, both)] = dot(p, vaug[g]).reshape(both, tokens, 2 * HD)
-            top[pl.ds(h, both)] = jnp.broadcast_to(m, (both, tokens, HD))
-            return 0
-
-        lax.fori_loop(0, per // both, step, 0)
-
-    half = groups // 2
-    for g in range(half):
-        pool_part(g)
+    pool_part(FIRST, SECOND)
 
     each(lambda o: two_in(o).wait_recv())
     paired(hidden, hid_other, 0).wait_recv()
@@ -274,8 +339,7 @@
         combined[h] = combined[h] + delta[:, h * vals : (h + 1) * vals]
     paired(combined.at[other], recvc, 1).start()
 
-    for g in range(half, groups):
-        pool_part(g)
+    pool_part(SECOND, steps)
 
     paired(combined.at[other], recvc, 1).wait_recv()
     each(lambda o: page_in(o).wait_recv())
@@ -284,7 +348,6 @@
     arrived = inst * page_tokens
     for g in range(groups):
         k2[g, :arrived, :] = in_pages[:, :, 2 * g * HD : (2 * g + 1) * HD].reshape(arrived, HD)
-        k2[g, arrived:, :] = new_keys[:, g * HD : (g + 1) * HD]
         v2[g, :arrived, :HD] = in_pages[:, :, (2 * g + 1) * HD : (2 * g + 2) * HD].reshape(
             arrived, HD
         )
@@ -310,24 +373,14 @@
     paired(combined.at[other], recvc, 1).wait_send()
 
 
-def shards(
-    hidden,
-    value_weight,
-    adapter_down,
-    adapter_up,
-    block_adapter,
-    queries,
-    new_keys,
-    kv_pool,
-    page_request,
-    page_pos,
-    token_request,
-    token_pos,
-    send_page,
-    send_dest,
-    dest_slot,
-    send_count,
-):
+def settle(attended, new_values, attended_out, new_values_out):
+    attended_out[...] = attended[...]
+    new_values_out[...] = new_values[...]
+
+
+def shards(*args):
+    hidden, value_weight, adapter_down = args[:3]
+    queries, new_keys, kv_pool = args[5:8]
     inst = lax.axis_size("inst")
     tokens, feats = hidden.shape
     rank, wide = adapter_down.shape
@@ -340,11 +393,7 @@
     tiles = (rank // 16) * (wide + kv_cols) // HD
     slots = -(-tiles // inst)
     last = inst * page_tokens + tokens
-    zero_p = jnp.zeros((6, pages), jnp.int32)
-    page_info = jnp.concatenate([page_request[None], page_pos[None], zero_p], axis=0)
-    zero_t = jnp.zeros((6, tokens), jnp.int32)
-    token_info = jnp.concatenate([token_request[None], token_pos[None], zero_t], axis=0)
-    smem = pl.BlockSpec(memory_space=pltpu.SMEM)
+    anywhere = pl.BlockSpec(memory_space=pl.ANY)
     vmem = pl.BlockSpec(memory_space=pltpu.VMEM)
     share = (inst, slots * 16, HD)
     out = pl.pallas_call(
@@ -353,9 +402,13 @@
             jax.ShapeDtypeStruct((tokens, heads * HD), BF16),
             jax.ShapeDtypeStruct((tokens, vals), BF16),
         ),
-        in_specs=[smem] * 5 + [vmem] * 9,
+        in_specs=[anywhere] * 16,
         out_specs=(vmem, vmem),
         scratch_shapes=[
+            (pltpu.SMEM if k in (4, 12, 13, 14, 15) else pltpu.VMEM)(a.shape, a.dtype)
+            for k, a in enumerate(args)
+        ]
+        + [
             pltpu.VMEM(share, BF16),
             pltpu.VMEM(share, BF16),
             pltpu.VMEM(share, BF16),
@@ -373,34 +426,29 @@
             pltpu.VMEM((groups, keys, 2 * HD), BF16),
             pltpu.VMEM((tokens, keys), F32),
             pltpu.VMEM((tokens, last), F32),
+            pltpu.VMEM((pages, keys), BF16),
             pltpu.VMEM((groups, last, HD), BF16),
             pltpu.VMEM((groups, last, 2 * HD), BF16),
             pltpu.VMEM((heads, tokens, 2 * HD), F32),
             pltpu.VMEM((heads, tokens, HD), F32),
         ]
         + [pltpu.SemaphoreType.DMA((inst,))] * 8
-        + [pltpu.SemaphoreType.DMA((2,))] * 2,
+        + [pltpu.SemaphoreType.DMA((2,))] * 2
+        + [pltpu.SemaphoreType.DMA((16,))],
         compiler_params=pltpu.CompilerParams(
             collective_id=0, has_side_effects=True, vmem_limit_bytes=56 * 1024 * 1024
         ),
         name="serve",
     )(
-        block_adapter,
-        send_page,
-        send_dest,
-        dest_slot,
-        send_count,
-        page_info,
-        token_info,
-        hidden,
-        value_weight,
-        adapter_down,
-        adapter_up,
-        queries,
-        new_keys,
-        kv_pool,
-    )
-    return out
+        *args
+    )
+    return pl.pallas_call(
+        settle,
+        out_shape=tuple(jax.ShapeDtypeStruct(a.shape, a.dtype) for a in out),
+        in_specs=[vmem] * 2,
+        out_specs=(vmem, vmem),
+        name="settle",
+    )(*out)
 
 
 def solution(mesh):

time: 43.4 us -> 35.1 us (0.81)
  the two profiles are of different devices: /device:TPU:15 before, /device:TPU:0 now
where the time goes in v1:
time: 35.1 us; the launch traced here: 34.9 us
  Pallas kernels  33.6 us (96%)
  between operations  1.29 us (4%)
    pallas_call x1, Pallas kernels, shards(): pl.pallas_call(functools.partial(kernel, inst), out_shape=(jax.ShapeDtype...  31.7 us
    pallas_call x1, Pallas kernels, shards(): pl.pallas_call(settle, out_shape=tuple((jax.ShapeDtypeStruct(a.shape, a.d...  1.88 us

profile of v1, /device:TPU:0, one launch (start us, length us, event | category | flops | bytes accessed | tf_op | source)
XLA Modules:
  0.0 34.9 jit_solution(5926031047510169630)
XLA Ops:
  1.3 31.7 %serve.1 = (bf16[128,2048]{1,0:T(8,128)(2,1)}, bf16[128,256]{1,0:T(8,128)(2,1)}) custom-call(bf16[128,1280]{1,0:T(8,128)(2,1)} %refs_0_.1, bf16[1280,512]{1,0:T(8,128)(2,1)} %refs_1_.1, bf16[32,2560]{1,0:T(8,128)(2,1)} %refs_2_.1, bf16[32,512]{1,0:T(8,128)(2,1)} %refs_3_.1, s32[8]{0:T(128)} %refs_4_.1, bf16[128,2048]{1,0:T(8,128)(2,1)} %refs_5_.1, ...), custom_call_target="tpu_custom_call" | custom-call | tf_op jit(solution)/shard_map/serve/pallas_call | solution.py:399
  33.0 1.9 %settle.1 = (bf16[128,2048]{1,0:T(8,128)(2,1)}, bf16[128,256]{1,0:T(8,128)(2,1)}) custom-call(bf16[128,2048]{1,0:T(8,128)(2,1)} %get-tuple-element.4.attended, bf16[128,256]{1,0:T(8,128)(2,1)} %get-tuple-element.5.new_values), custom_call_target="tpu_custom_call" | custom-call | tf_op jit(solution)/shard_map/settle/pallas_call | solution.py:445

commit v2 on v1

--- a/solution.py
+++ b/solution.py
@@ -10,8 +10,8 @@
 
 HD = 128
 FAR = -1e30
-FIRST = 3
-SECOND = 6
+FIRST = 1
+SECOND = 3
 F32 = jnp.float32
 BF16 = jnp.bfloat16
 MESH = pl.DeviceIdType.MESH
@@ -232,9 +232,10 @@
     owners = owners.astype(BF16)
     indices = indices.astype(BF16)
     spread_page = lax.broadcasted_iota(jnp.int32, (pages, keys), 0)
-    spread_key = lax.broadcasted_iota(jnp.int32, (pages, keys), 1) // page_tokens
-    spread[...] = (spread_page == spread_key).astype(F32).astype(BF16)
-    entry = lax.broadcasted_iota(jnp.int32, (1, keys), 1) % page_tokens
+    spread_key = lax.broadcasted_iota(jnp.int32, (pages, keys), 1)
+    inside = spread_key - spread_page * page_tokens
+    spread[...] = ((inside >= 0) & (inside < page_tokens)).astype(F32).astype(BF16)
+    entry = lax.broadcasted_iota(jnp.int32, (1, keys), 1) & (page_tokens - 1)
     key_at = dot(indices, spread[...])[0:1] * page_tokens + entry.astype(F32)
     ok = (dot(owners, spread[...])[0:1] == t_req) & (key_at <= t_pos)
     bias[...] = jnp.where(ok, 0.0, FAR)
@@ -265,18 +266,18 @@
     for b in range(inst // per_row):
         row = jnp.full((1, HD), -1, jnp.int32)
         for j in range(per_row):
-            row = jnp.where(lane // page_tokens == j, in_slots[b * per_row + j][0:1], row)
+            row = jnp.where((lane >= j * page_tokens) & (lane < (j + 1) * page_tokens), in_slots[b * per_row + j][0:1], row)
         match = (page_col == row).astype(F32).astype(BF16)
         gone = gone + dot_t(jnp.ones((8, HD), BF16), match)
         req = jnp.where(row >= 0, dot(owners, match)[0:1], -2.0)
-        at = dot(indices, match)[0:1] * page_tokens + (lane % page_tokens).astype(F32)
+        at = dot(indices, match)[0:1] * page_tokens + (lane & (page_tokens - 1)).astype(F32)
         ok = (req == t_req) & (at <= t_pos)
         bias2[:, b * HD : (b + 1) * HD] = jnp.where(ok, 0.0, FAR)
     gone = (gone > 0.5).astype(F32).astype(BF16)
     lost = dot(gone, spread[...])[0:1] > 0.5
     bias[...] = jnp.where(lost, FAR, bias[...])
 
-    both = 2
+    both = 4
 
     def pool_part(lo, hi):
         def step(i, _):

time: 35.1 us -> 34.7 us (0.989)
  no operation moved by 1% of the time
where the time goes in v2:
time: 34.7 us; the launch traced here: 34.6 us
  Pallas kernels  33.3 us (96%)
  between operations  1.29 us (4%)
    pallas_call x1, Pallas kernels, shards(): pl.pallas_call(functools.partial(kernel, inst), out_shape=(jax.ShapeDtype...  31.4 us
    pallas_call x1, Pallas kernels, shards(): pl.pallas_call(settle, out_shape=tuple((jax.ShapeDtypeStruct(a.shape, a.d...  1.88 us

profile of v2, /device:TPU:0, one launch (start us, length us, event | category | flops | bytes accessed | tf_op | source)
XLA Modules:
  0.0 34.6 jit_solution(17915536691205116797)
XLA Ops:
  1.3 31.4 %serve.1 = (bf16[128,2048]{1,0:T(8,128)(2,1)}, bf16[128,256]{1,0:T(8,128)(2,1)}) custom-call(bf16[128,1280]{1,0:T(8,128)(2,1)} %refs_0_.1, bf16[1280,512]{1,0:T(8,128)(2,1)} %refs_1_.1, bf16[32,2560]{1,0:T(8,128)(2,1)} %refs_2_.1, bf16[32,512]{1,0:T(8,128)(2,1)} %refs_3_.1, s32[8]{0:T(128)} %refs_4_.1, bf16[128,2048]{1,0:T(8,128)(2,1)} %refs_5_.1, ...), custom_call_target="tpu_custom_call" | custom-call | tf_op jit(solution)/shard_map/serve/pallas_call | solution.py:400
  32.7 1.9 %settle.1 = (bf16[128,2048]{1,0:T(8,128)(2,1)}, bf16[128,256]{1,0:T(8,128)(2,1)}) custom-call(bf16[128,2048]{1,0:T(8,128)(2,1)} %get-tuple-element.4.attended, bf16[128,256]{1,0:T(8,128)(2,1)} %get-tuple-element.5.new_values), custom_call_target="tpu_custom_call" | custom-call | tf_op jit(solution)/shard_map/settle/pallas_call | solution.py:446
